TPU v7x, 512 devices: a whole 4x4x16 slice. The times are simulated.
512 devices in a mesh: dp: 16 (over z), pair: 32 (over y, x, core).
Axes of the slice: x: 4, y: 4, z: 16, core: 2. Of those that a mesh axis runs over, the one named last changes fastest.
Arguments:
- embeddings: bfloat16 [16384, 768], P('dp'), may hold values from -4 to 4
- block_sizes: int32 [128], replicated, may hold values from 1 to 128
- fetch_blocks: int32 [16, 32, 16], P('dp', 'pair'), may hold values from 0 to 7
- partners: int32 [16, 32, 16, 4], P('dp', 'pair'), may hold values from 0 to 7, as said below
Outputs:
- weighted_sums: float32 [16384, 768], P(('dp', 'pair'))
- log_mass: float32 [16384], P(('dp', 'pair'))
Inputs may be any that keep to these rules, and one draw needn't show every extreme that they name: `partners`: the 4 entries of one worker and owner are different blocks.
All inputs are finite; a program needn't handle non-finite values.
Results may differ from a plain program's by a relative error of at most 0.002.
Values may be sent and summed in bfloat16 or wider, within the bound.
A program may use at most 64 MiB of HBM per device.

v0:
```python
import jax
import jax.numpy as jnp
from jax import lax
from jax.sharding import PartitionSpec as P

inv_band = 1.0


def body(embeddings, block_sizes, fetch_blocks, partners):
    owners = lax.axis_size("dp")
    mine = lax.axis_index("dp")
    rows, width = embeddings.shape
    count = block_sizes.shape[0] // owners
    depth = rows // count
    blocks = embeddings.reshape(count, depth, width)
    wanted = fetch_blocks.reshape(owners)
    links = partners.reshape(owners, partners.shape[-1])
    lanes = jnp.arange(depth, dtype=jnp.int32)
    sizes_all = block_sizes.reshape(owners, count)
    live_all = (lanes[None, None, :] < sizes_all[:, :, None]).astype(jnp.float32)
    local_live = lax.dynamic_index_in_dim(live_all, mine, 0, keepdims=False)
    far_live = live_all[jnp.arange(owners), wanted]
    local_norms = jnp.sum(jnp.square(blocks.astype(jnp.float32)), axis=2)
    asked = lax.all_to_all(
        wanted.reshape(owners, 1), "dp", split_axis=0, concat_axis=0, tiled=True
    ).reshape(owners)
    sending = blocks[asked]
    fetched = lax.all_to_all(sending, "dp", split_axis=0, concat_axis=0, tiled=True)
    far_norms = jnp.sum(jnp.square(fetched.astype(jnp.float32)), axis=2)

    def visit(carry, item):
        near_acc, near_mass = carry
        far_block, far_norm, far_mask, picked = item
        near_blocks = blocks[picked]
        dots = jnp.einsum("pie,je->pij", near_blocks, far_block, preferred_element_type=jnp.float32)
        dist = local_norms[picked][:, :, None] + far_norm[None, None, :] - 2.0 * dots
        kern = jnp.exp(-inv_band * dist) * local_live[picked][:, :, None] * far_mask[None, None, :]
        weights = kern.astype(jnp.bfloat16)
        near_sum = jnp.einsum("pij,je->pie", weights, far_block, preferred_element_type=jnp.float32)
        far_sum = jnp.einsum(
            "pij,pie->je", weights, near_blocks, preferred_element_type=jnp.float32
        )
        near_acc = near_acc.at[picked].add(near_sum)
        near_mass = near_mass.at[picked].add(jnp.sum(kern, axis=2))
        return ((near_acc, near_mass), (far_sum, jnp.sum(kern, axis=(0, 1))))

    start = (jnp.zeros((count, depth, width), jnp.float32), jnp.zeros((count, depth), jnp.float32))
    (near_acc, near_mass), (far_sums, far_mass) = lax.scan(
        visit, start, (fetched, far_norms, far_live, links)
    )
    back_sums, back_mass = (
        lax.all_to_all(
            far_sums.astype(jnp.bfloat16), "dp", split_axis=0, concat_axis=0, tiled=True
        ).astype(far_sums.dtype),
        lax.all_to_all(
            far_mass.astype(jnp.bfloat16), "dp", split_axis=0, concat_axis=0, tiled=True
        ).astype(far_mass.dtype),
    )
    near_acc = near_acc.at[asked].add(back_sums)
    near_mass = near_mass.at[asked].add(back_mass)
    total, mass = (
        lax.psum_scatter(near_acc.reshape(rows, width), "pair", scatter_dimension=0, tiled=True),
        lax.psum_scatter(near_mass.reshape(rows), "pair", scatter_dimension=0, tiled=True),
    )
    return (total, jnp.log(1.0 + mass))


def solution(mesh):
    return jax.shard_map(
        body,
        mesh=mesh,
        in_specs=(P("dp", None), P(), P("dp", "pair", None), P("dp", "pair", None, None)),
        out_specs=(P(("dp", "pair"), None), P(("dp", "pair"))),
        check_vma=False,
    )
```

profile of v0, /device:TPU:1, one launch (start us, length us, event | category | flops | bytes accessed | tf_op | source)
XLA Modules:
  0.0 635.8 jit_solution(1445776189362782371)
XLA Ops:
  7.9 26.8 %all_to_all.31 = s32[16,1,1]{2,1,0:T(1,128)S(1)} all-to-all(s32[16,1,1]{2,1,0:T(1,128)S(1)} %copy.14), channel_id=1, replica_groups=mesh['dp'=16,'pair'=32] {'dp'}, dimensions={0} | all-to-all | bytes 128 | tf_op jit(solution)/shard_map/all_to_all | solution.py:24
  35.1 3.9 gather_fusion.3
  39.0 4.6 all-to-all-start.1
  44.6 1.8 multiply_reduce_fusion.1
  46.4 133.9 %all-to-all-done.1 = bf16[16,128,768]{2,1,0:T(8,128)(2,1)} async-done(((bf16[16,128,768]{2,1,0:T(8,128)(2,1)}), bf16[16,128,768]{2,1,0:T(8,128)(2,1)}, u32[]{:S(2)}, u32[]{:S(2)}) %all-to-all-start.1) | async-done | bytes 3145760 | tf_op jit(solution)/shard_map/all_to_all | solution.py:28
  180.3 2.6 multiply_reduce_fusion
  182.9 2.0 broadcast_in_dim.14
  184.9 179.1 %while.16 = (s32[]{:T(128)}, f32[8,128,768]{2,1,0:T(8,128)}, f32[8,128]{1,0:T(8,128)S(1)}, bf16[16,128,768]{2,1,0:T(8,128)(2,1)}, bf16[16,128]{1,0:T(8,128)(2,1)...) while((s32[]{:T(128)}, f32[8,128,768]{2,1,0:T(8,128)}, ...), condition=%wide.region_7.8_spmd, body=%wide.region_2.7_spmd.sunk | while | flops 302973824 | bytes 10647057 | solution.py:48
  184.9 2.0 gather_fusion.1
  188.0 1.4 fusion.48
  190.7 3.7 scatter_fusion
  196.1 2.0 gather_fusion.1
  199.2 1.4 fusion.48
  201.9 3.7 scatter_fusion
  207.3 2.0 gather_fusion.1
  210.4 1.4 fusion.48
  213.1 3.7 scatter_fusion
  218.5 2.0 gather_fusion.1
  221.6 1.4 fusion.48
  224.3 3.7 scatter_fusion
  229.7 2.0 gather_fusion.1
  232.8 1.4 fusion.48
  235.5 3.7 scatter_fusion
  240.9 2.0 gather_fusion.1
  244.0 1.4 fusion.48
  246.7 3.7 scatter_fusion
  252.0 2.0 gather_fusion.1
  255.2 1.4 fusion.48
  257.9 3.7 scatter_fusion
  263.2 2.0 gather_fusion.1
  266.4 1.4 fusion.48
  269.0 3.7 scatter_fusion
  274.4 2.0 gather_fusion.1
  277.5 1.4 fusion.48
  280.2 3.7 scatter_fusion
  285.5 2.0 gather_fusion.1
  288.7 1.4 fusion.48
  291.4 3.8 scatter_fusion
  296.8 2.0 gather_fusion.1
  299.9 1.4 fusion.48
  302.6 3.7 scatter_fusion
  308.0 2.0 gather_fusion.1
  311.1 1.4 fusion.48
  313.8 3.7 scatter_fusion
  319.2 2.0 gather_fusion.1
  322.3 1.4 fusion.48
  325.0 3.7 scatter_fusion
  330.4 2.0 gather_fusion.1
  333.5 1.4 fusion.48
  336.2 3.7 scatter_fusion
  341.6 2.0 gather_fusion.1
  344.7 1.4 fusion.48
  347.4 3.7 scatter_fusion
  352.8 2.0 gather_fusion.1
  356.0 1.4 fusion.48
  358.7 3.7 scatter_fusion
  364.0 146.7 %all_to_all.32 = bf16[16,128,768]{2,1,0:T(8,128)(2,1)S(1)} all-to-all(bf16[16,128,768]{2,1,0:T(8,128)(2,1)} %get-tuple-element.68), channel_id=1, replica_groups=mesh['dp'=16,'pair'=32] {'dp'}, dimensions={0} | all-to-all | bytes 6291456 | tf_op jit(solution)/shard_map/all_to_all | solution.py:52
  510.7 3.3 convert_element_type.32
  514.0 9.3 %scatter_fusion.2 = f32[8,128,768]{2,1,0:T(8,128)S(1)} fusion(f32[8,128,768]{2,1,0:T(8,128)S(1)} %copy-done, s32[16]{0:T(128)S(1)} %fusion.20, f32[16,128,768]{2,1,0:T(8,128)} %convert_element_type.32), kind=kCustom, calls=%fused_computation.7 | custom fusion | flops 1572864 | bytes 18874432 | tf_op jit(solution)/shard_map/scatter-add | solution.py:59
  523.3 1.7 copy-done.1
  525.6 12.5 %all-to-all-start.3 = ((bf16[16,1,128]{2,1,0:T(2,128)(2,1)}), bf16[16,1,128]{2,1,0:T(2,128)(2,1)S(1)}, u32[]{:S(2)}, u32[]{:S(2)}) async-start(bf16[16,1,128]{2,1,0:T(2,128)(2,1)} %copy.16), calls=%async_computation.4 | async-start | bytes 16384 | tf_op jit(solution)/shard_map/all_to_all | solution.py:55
  540.1 9.3 %all-to-all-done.3 = bf16[16,1,128]{2,1,0:T(2,128)(2,1)S(1)} async-done(((bf16[16,1,128]{2,1,0:T(2,128)(2,1)}), bf16[16,1,128]{2,1,0:T(2,128)(2,1)S(1)}, u32[]{:S(2)}, u32[]{:S(2)}) %all-to-all-start.3) | async-done | bytes 4128 | tf_op jit(solution)/shard_map/all_to_all | solution.py:55
  550.0 64.6 %all-reduce = f32[1024]{0:T(1024)S(1)} all-reduce(f32[1024]{0:T(1024)S(1)} %bitcast.76), channel_id=3, replica_groups=mesh['dp'=16,'pair'=32] {'pair'}, use_global_device_ids=true, to_apply=%region_11.12.clone | all-reduce | flops 1024 | bytes 8192
  615.2 13.7 %reduce-scatter.2.cloned.1.call-done = f32[32,768]{1,0:T(8,128)} async-done(((f32[1024,768]{1,0:T(8,128)}), f32[32,768]{1,0:T(8,128)}) %reduce-scatter.2.cloned.1.call-update) | async-done | bytes 98320 | tf_op jit(solution)/shard_map/reduce_scatter | solution.py:62
  (173 shorter events, 69.5 us)
Async XLA Ops:
  39.0 4.7 copy-start.3
  39.0 4.8 copy-start.2
  39.0 4.9 copy-start.4
  39.0 141.3 %all-to-all-start.1 = ((bf16[16,128,768]{2,1,0:T(8,128)(2,1)}), bf16[16,128,768]{2,1,0:T(8,128)(2,1)}, u32[]{:S(2)}, u32[]{:S(2)}) async-start(bf16[16,128,768]{2,1,0:T(8,128)(2,1)} %gather_fusion.3), calls=%async_computation.1 | async-start | bytes 6291456 | tf_op jit(solution)/shard_map/all_to_all | solution.py:28
  43.6 585.4 %reduce-scatter.2.cloned.1.call-start = ((), (), s32[]{:S(2)}) async-start(), calls=%async_computation.5 | async-start | bytes 3244032 | tf_op jit(solution)/shard_map/reduce_scatter | solution.py:62
  510.7 3.3 copy-start
  523.3 1.7 copy-start.1
  525.6 23.8 %all-to-all-start.3 = ((bf16[16,1,128]{2,1,0:T(2,128)(2,1)}), bf16[16,1,128]{2,1,0:T(2,128)(2,1)S(1)}, u32[]{:S(2)}, u32[]{:S(2)}) async-start(bf16[16,1,128]{2,1,0:T(2,128)(2,1)} %copy.16), calls=%async_computation.4 | async-start | bytes 16384 | tf_op jit(solution)/shard_map/all_to_all | solution.py:55
Sparse Core Ops, SparseCore 0:
  525.1 103.7 reduce-scatter.1
where the time goes:
time: 639 us; the launch traced here: 636 us
  blocking collectives  238 us (37%)
  waiting for transfers between devices  157 us (25%)
  other arithmetic  87.8 us (14%)
  local copies, waits for them, and re-layouts  61.6 us (10%)
  matrix products  58.5 us (9%)
  starting transfers between devices  17.2 us (3%)
  between operations  14.8 us (2%)
    all_to_all x1, blocking collectives, body(): lax.all_to_all(far_sums.astype(jnp.bfloat16), 'dp', split_axis=0, concat_...  147 us
    all_to_all x1, waiting for transfers between devices, body(): lax.all_to_all(sending, 'dp', split_axis=0, concat_axis=0, tiled=True)  134 us
    unnamed x1, blocking collectives  64.6 us
    scatter-add x16, other arithmetic, visit(): near_acc = near_acc.at[picked].add(near_sum)  59.3 us
    gather x16, local copies, waits for them, and re-layouts, visit(): near_blocks = blocks[picked]  32.1 us
    all_to_all x1, blocking collectives, body(): lax.all_to_all(wanted.reshape(owners, 1), 'dp', split_axis=0, concat_axis...  26.8 us
    dot_general x16, matrix products, visit(): jnp.einsum('pie,je->pij', near_blocks, far_block, preferred_element_type=...  22.5 us
    dot_general x16, matrix products, visit(): jnp.einsum('pij,je->pie', weights, far_block, preferred_element_type=jnp....  20.4 us
  transfers between devices with their start and end apart: 3, of which 3 were waited for; matrix products, arithmetic and copies ran while one was open for 1% of the time, Pallas kernels for 0%

commit v1 on v0

v1 whole, which is shorter than its diff:
```python
import jax
import jax.numpy as jnp
from jax import lax
from jax.experimental import pallas as pl
from jax.experimental.pallas import tpu as pltpu
from jax.sharding import PartitionSpec as P

MESH = pl.DeviceIdType.MESH
F32, BF16, I32 = jnp.float32, jnp.bfloat16, jnp.int32

OWNERS, COUNT, DEPTH, WIDTH = 16, 8, 128, 768
SIDE = 4
CHIPS = SIDE * SIDE
SHARD = 32
ROWS = CHIPS * SHARD
PAIR = 2 * SHARD
GROUP = 4
COLS = GROUP * PAIR
WIDE = WIDTH + 128
FAR = 1e30

KIDS = {0: (2, 1), 2: (5, 3), 5: (8, 7, 4, 6)}
SLOTS = (0, 2, -2, 1, -1, 5, -5, 3, -3, 8, 7, -7, 4, -4, 6, -6)
SLOT = {d: s for s, d in enumerate(SLOTS)}
SLOT[-8] = SLOT[8]
REACH = 3
EDGES = {}
for parent, kids in KIDS.items():
    for kid in kids:
        for sign in (1, -1):
            EDGES[sign * kid] = sign * parent
EDGE = {d: e for e, d in enumerate(EDGES)}


def below(parent):
    sign = -1 if parent < 0 else 1
    kids = KIDS.get(abs(parent), ())
    if parent == 0:
        return [s * k for k in kids for s in (1, -1)]
    return [sign * k for k in kids]


OFFSETS = [(dx, dy) for dy in (2, 1, 3, 0) for dx in (2, 1, 3, 0)]
PEERS = [o for o in OFFSETS if o != (0, 0)]


def kernel(emb, bs_hbm, fetch_hbm, part_hbm, out_ref, log_ref, xz, cols, kern, acc, mass, ni, sizes, fetch, part,
           mown, mpair, mplane, cm, sg, send, recv, loc_sem, e_send, e_recv, d_send, d_recv, c_send, c_recv,
           m_send, m_recv, r_send, r_recv):
    z = lax.axis_index("dp")
    p = lax.axis_index("pair")
    core = lax.rem(p, 2)
    chip = p // 2
    x = lax.rem(chip, SIDE)
    y = chip // SIDE
    half = chip // 2

    def along(d):
        return (lax.rem(z + d + OWNERS, OWNERS), p)

    def place(dx, dy):
        return lax.rem(y + dy, SIDE) * SIDE + lax.rem(x + dx, SIDE)

    def peer(dx, dy):
        return (z, place(dx, dy) * 2 + core)

    other = (z, chip * 2 + 1 - core)

    barrier = pltpu.get_barrier_semaphore()
    for d in range(1, REACH + 1):
        for s in (1, -1):
            pl.semaphore_signal(barrier, 1, device_id=along(s * d), device_id_type=MESH)
    for dx, dy in PEERS:
        pl.semaphore_signal(barrier, 1, device_id=peer(dx, dy), device_id_type=MESH)
    pl.semaphore_signal(barrier, 1, device_id=other, device_id_type=MESH)

    loads = [
        pltpu.make_async_copy(fetch_hbm, fetch, loc_sem.at[0]),
        pltpu.make_async_copy(part_hbm, part, loc_sem.at[1]),
        pltpu.make_async_copy(bs_hbm, sizes, loc_sem.at[2]),
        pltpu.make_async_copy(emb.at[:, core], xz, loc_sem.at[3]),
        pltpu.make_async_copy(emb.at[chip, core], cols.at[0, 0], loc_sem.at[4]),
        pltpu.make_async_copy(emb.at[chip, 1 - core], cols.at[0, 1], loc_sem.at[5]),
    ]
    for c in loads:
        c.start()
    pl.semaphore_wait(barrier, 2 * REACH + len(PEERS) + 1)

    sent = []

    def go(c):
        c.start()
        sent.append(c)

    def span(d):
        return (0, 16) if d == 8 else (16, 16) if d == -8 else (0, SHARD)

    def rows_copy(d):
        parent = EDGES[d]
        r0, nr = span(d)
        src = emb.at[chip, core, pl.ds(r0, nr)] if parent == 0 else cols.at[SLOT[parent], 0, pl.ds(r0, nr)]
        return pltpu.make_async_remote_copy(
            src_ref=src, dst_ref=cols.at[SLOT[d], 0, pl.ds(r0, nr)], send_sem=e_send.at[EDGE[d]],
            recv_sem=e_recv.at[EDGE[d]], device_id=along(d - parent), device_id_type=MESH)

    def twin_copy(s):
        return pltpu.make_async_remote_copy(
            src_ref=cols.at[s, 0], dst_ref=cols.at[s, 1], send_sem=d_send.at[s], recv_sem=d_recv.at[s],
            device_id=other, device_id_type=MESH)

    def count_copy(d):
        parent = EDGES[d]
        return pltpu.make_async_remote_copy(
            src_ref=cm.at[SLOT[parent]], dst_ref=cm.at[SLOT[d]], send_sem=c_send.at[EDGE[d]],
            recv_sem=c_recv.at[EDGE[d]], device_id=along(d - parent), device_id_type=MESH)

    def rows_in(*ds):
        for d in ds:
            rows_copy(d).wait_recv()
            for k in below(d):
                go(rows_copy(k))
        for d in ds:
            if d != 8:
                go(twin_copy(SLOT[d]))

    def counts_in(*ds):
        for d in ds:
            count_copy(d).wait_recv()
            for k in below(d):
                if k != -8:
                    go(count_copy(k))

    for d in below(0):
        go(rows_copy(d))

    sub8 = lax.broadcasted_iota(I32, (COUNT, 128), 0)
    lane8 = lax.broadcasted_iota(I32, (COUNT, 128), 1)
    loads[0].wait()
    loads[1].wait()
    hits = jnp.zeros((COUNT, 128), F32)
    for o in range(OWNERS):
        near = sub8 == part[0, 0, o, 0]
        for k in range(1, 4):
            near = jnp.logical_or(near, sub8 == part[0, 0, o, k])
        far = lane8 == o * COUNT + fetch[0, 0, o]
        hits = hits + jnp.where(jnp.logical_and(near, far), 1.0, 0.0)
    mown[...] = hits
    swap = pltpu.make_async_remote_copy(
        src_ref=mown, dst_ref=mpair, send_sem=m_send.at[15], recv_sem=m_recv.at[15], device_id=other,
        device_id_type=MESH)
    go(swap)
    swap.wait_recv()
    mplane[15] = mown[...] + mpair[...]
    plane = []
    for i, (dx, dy) in enumerate(PEERS):
        c = pltpu.make_async_remote_copy(
            src_ref=mplane.at[15], dst_ref=mplane.at[i], send_sem=m_send.at[i], recv_sem=m_recv.at[i],
            device_id=peer(dx, dy), device_id_type=MESH)
        go(c)
        plane.append(c)

    for c in loads[2:]:
        c.wait()
    bs = sizes[...].astype(F32)

    def row_norms(k, carry):
        v = xz[pl.ds(k * 4, 4)].reshape(4 * SHARD, WIDTH).astype(F32)
        n = jnp.sum(v * v, axis=1, keepdims=True)
        t = k * 4 * SHARD + lax.broadcasted_iota(I32, (4 * SHARD, 128), 0)
        lane = lax.broadcasted_iota(I32, (4 * SHARD, 128), 1)
        block = z * COUNT + t // PAIR
        size = jnp.sum(jnp.where(lane == block, bs, 0.0), axis=1, keepdims=True)
        inside = lax.rem(t // SHARD, 2) * PAIR + core * SHARD + lax.rem(t, SHARD)
        dead = inside.astype(F32) >= size
        ni[pl.ds(k * 4 * SHARD, 4 * SHARD)] = n + jnp.where(dead, FAR, 0.0)
        return carry

    lax.fori_loop(0, CHIPS // 4, row_norms, 0)

    lane1 = lax.broadcasted_iota(I32, (1, 128), 1)
    sub128 = lax.broadcasted_iota(I32, (128, 128), 0)
    lane128 = lax.broadcasted_iota(I32, (128, 128), 1)
    row64 = lax.broadcasted_iota(I32, (PAIR, 128), 0)
    mine = row64 < SHARD
    inside64 = lax.rem(chip, 2) * PAIR + jnp.where(mine, core * SHARD + row64, (1 - core) * SHARD + row64 - SHARD)
    inside64 = inside64.astype(F32)

    def block_of(d):
        return lax.rem(z - d + 2 * OWNERS, OWNERS) * COUNT + half

    def far_norms(g):
        parts = []
        for h in range(GROUP // 2):
            two = []
            for s in (g * GROUP + 2 * h, g * GROUP + 2 * h + 1):
                v = cols[s].reshape(PAIR, WIDTH).astype(F32)
                n = jnp.sum(v * v, axis=1, keepdims=True)
                size = jnp.sum(jnp.where(lane1 == block_of(SLOTS[s]), bs, 0.0), axis=1, keepdims=True)
                two.append(n + jnp.where(inside64 >= size, FAR, 0.0))
            n = jnp.concatenate(two, axis=0)
            parts.append(jnp.sum(jnp.where(sub128 == lane128, n, 0.0), axis=0, keepdims=True))
        return jnp.concatenate(parts, axis=1)

    def near(g):
        for s in range(g * GROUP, (g + 1) * GROUP):
            if s:
                twin_copy(s).wait_recv()
        far = cols[pl.ds(g * GROUP, GROUP)].reshape(COLS, WIDTH)
        nj = far_norms(g)

        def part_of(k, carry):
            r = pl.ds(k * 128, 128)
            v = xz[pl.ds(k * 4, 4)].reshape(128, WIDTH)
            dots = lax.dot_general(v, far, (((1,), (1,)), ((), ())), preferred_element_type=F32)
            n = ni[r]
            dist = jnp.concatenate([n, n], axis=1) + nj - 2.0 * dots
            kern[g, r] = jnp.exp(-dist)
            return carry

        lax.fori_loop(0, ROWS // 128, part_of, 0)

    def counts(g):
        out = []
        for h in range(GROUP // 2):
            two = []
            for s in (g * GROUP + 2 * h, g * GROUP + 2 * h + 1):
                there = cm[s, pl.ds(half, 1), :]
                here = jnp.where(lane8 == block_of(SLOTS[s]), cm[0], 0.0)
                both = here + jnp.where(lane8 == z * COUNT + sub8, there, 0.0)
                two.append(jnp.sum(both, axis=1, keepdims=True))
            out.append(jnp.where(lane8 < PAIR, two[0], two[1]))
        sg[g] = jnp.concatenate(out, axis=1)

    def part_sums(g, r0):
        r = pl.ds(r0, 128)
        k = kern[g, r]
        b0 = r0 // PAIR
        s0 = jnp.broadcast_to(sg[g, pl.ds(b0, 1), :], (PAIR, COLS))
        s1 = jnp.broadcast_to(sg[g, pl.ds(b0 + 1, 1), :], (PAIR, COLS))
        s = jnp.concatenate([s0, s1], axis=0)
        w = s * k.astype(BF16).astype(F32)
        hi = w.astype(BF16)
        lo = (w - hi.astype(F32)).astype(BF16)
        far = cols[pl.ds(g * GROUP, GROUP)].reshape(COLS, WIDTH)
        t = jnp.dot(hi, far, preferred_element_type=F32) + jnp.dot(lo, far, preferred_element_type=F32)
        m = s * k
        m = m[:, :128] + m[:, 128:]
        if g:
            t = t + acc[r]
            m = m + mass[r]
        return t, m

    def sums(g):
        def step(k, carry):
            t, m = part_sums(g, k * 128)
            acc[pl.ds(k * 128, 128)] = t
            mass[pl.ds(k * 128, 128)] = m
            return carry

        lax.fori_loop(0, ROWS // 128, step, 0)

    rows_in(2, -2)
    rows_in(1, -1)
    total = mplane[15]
    for i, c in enumerate(plane):
        c.wait_recv()
        total = total + mplane[i]
    cm[0] = total
    for d in below(0):
        go(count_copy(d))
    near(0)
    rows_in(5, -5)
    rows_in(3, -3)
    counts_in(2, -2, 1, -1)
    counts(0)
    sums(0)
    near(1)
    rows_in(8, -8)
    rows_in(7, -7)
    counts_in(5, -5, 3, -3)
    counts(1)
    sums(1)
    near(2)
    rows_in(4, -4)
    rows_in(6, -6)
    near(3)
    counts_in(8, 7, -7, 4, -4, 6, -6)
    counts(2)
    sums(2)
    counts(3)

    lane32 = lax.broadcasted_iota(I32, (SHARD, 128), 1)
    order = []
    i = 0
    for dy in (2, 1, 3, 0):
        row = lax.rem(y + dy, SIDE)
        t, m = part_sums(3, row * 128)
        acc[pl.ds(row * 128, 128)] = t
        mass[pl.ds(row * 128, 128)] = m
        for dx in (2, 1, 3, 0):
            if (dx, dy) == (0, 0):
                continue
            q = place(dx, dy) * SHARD
            v = acc[pl.ds(q, SHARD)]
            a = jnp.sum(mass[pl.ds(q, SHARD)], axis=1, keepdims=True)
            a0 = a.astype(BF16)
            rest = a - a0.astype(F32)
            a1 = rest.astype(BF16)
            a2 = (rest - a1.astype(F32)).astype(BF16)
            send[i, :, :WIDTH] = v.astype(BF16)
            tail = jnp.where(lane32 == 0, a0.astype(F32),
                             jnp.where(lane32 == 1, a1.astype(F32), jnp.where(lane32 == 2, a2.astype(F32), 0.0)))
            send[i, :, WIDTH:] = tail.astype(BF16)
            c = pltpu.make_async_remote_copy(
                src_ref=send.at[i], dst_ref=recv.at[i], send_sem=r_send.at[i], recv_sem=r_recv.at[i],
                device_id=peer(dx, dy), device_id_type=MESH)
            go(c)
            order.append(c)
            i += 1

    q = chip * SHARD
    v = acc[pl.ds(q, SHARD)]
    a = mass[pl.ds(q, SHARD)]
    for i, c in enumerate(order):
        c.wait_recv()
        v = v + recv[i, :, :WIDTH].astype(F32)
        a = a + recv[i, :, WIDTH:].astype(F32)
    out_ref[...] = v
    m = jnp.log(1.0 + jnp.sum(a, axis=1, keepdims=True))
    sub32 = lax.broadcasted_iota(I32, (SHARD, 128), 0)
    log_ref[...] = jnp.sum(jnp.where(sub32 == lane32, m, 0.0), axis=0, keepdims=True)
    for c in sent:
        c.wait_send()


def body(embeddings, block_sizes, fetch_blocks, partners):
    hbm = pl.BlockSpec(memory_space=pl.ANY)
    vmem = pl.BlockSpec(memory_space=pltpu.VMEM)
    dma = pltpu.SemaphoreType.DMA
    edges = len(EDGES)
    out, logs = pl.pallas_call(
        kernel,
        out_shape=(jax.ShapeDtypeStruct((SHARD, WIDTH), F32), jax.ShapeDtypeStruct((1, 128), F32)),
        in_specs=[hbm] * 4,
        out_specs=(vmem, vmem),
        scratch_shapes=[
            pltpu.VMEM((CHIPS, SHARD, WIDTH), BF16),
            pltpu.VMEM((OWNERS, 2, SHARD, WIDTH), BF16),
            pltpu.VMEM((OWNERS // GROUP, ROWS, COLS), F32),
            pltpu.VMEM((ROWS, WIDTH), F32),
            pltpu.VMEM((ROWS, 128), F32),
            pltpu.VMEM((ROWS, 128), F32),
            pltpu.VMEM((1, 128), I32),
            pltpu.SMEM((1, 1, 16), I32),
            pltpu.SMEM((1, 1, 16, 4), I32),
            pltpu.VMEM((COUNT, 128), F32),
            pltpu.VMEM((COUNT, 128), F32),
            pltpu.VMEM((CHIPS, COUNT, 128), F32),
            pltpu.VMEM((OWNERS, COUNT, 128), F32),
            pltpu.VMEM((OWNERS // GROUP, COUNT, COLS), F32),
            pltpu.VMEM((len(PEERS), SHARD, WIDE), BF16),
            pltpu.VMEM((len(PEERS), SHARD, WIDE), BF16),
            dma((6,)),
            dma((edges,)), dma((edges,)),
            dma((OWNERS,)), dma((OWNERS,)),
            dma((edges,)), dma((edges,)),
            dma((CHIPS,)), dma((CHIPS,)),
            dma((CHIPS,)), dma((CHIPS,)),
        ],
        compiler_params=pltpu.CompilerParams(collective_id=0, has_side_effects=True, vmem_limit_bytes=40 << 20),
        cost_estimate=pl.CostEstimate(flops=3 * 2 * 512 * 1024 * 768, bytes_accessed=4 << 20, transcendentals=512 * 1024),
    )(embeddings.reshape(CHIPS, 2, SHARD, WIDTH), block_sizes.reshape(1, -1), fetch_blocks, partners)
    return out, logs[0, :SHARD]


def solution(mesh):
    return jax.shard_map(
        body,
        mesh=mesh,
        in_specs=(P("dp", None), P(), P("dp", "pair", None), P("dp", "pair", None, None)),
        out_specs=(P(("dp", "pair"), None), P(("dp", "pair"))),
        check_vma=False,
    )
```

time: 639 us -> 59.5 us (0.09)
  blocking collectives: 238 us -> 0 us
  waiting for transfers between devices: 157 us -> 0 us
  other arithmetic: 87.8 us -> 0 us
  matrix products: 58.5 us -> 0 us
  local copies, waits for them, and re-layouts: 61.6 us -> 4.63 us
  Pallas kernels: 0 us -> 54.1 us
  starting transfers between devices: 17.2 us -> 0 us
  between operations: 14.8 us -> 0.64 us
    all_to_all x2 -> x0, blocking collectives: 174 us -> none  [the longest x1 147 us: body(): lax.all_to_all(far_sums.astype(jnp.bfloat16), 'dp', split_axis=0, concat_...]
    all_to_all x2 -> x0, waiting for transfers between devices: 143 us -> none  [the longest x1 134 us: body(): lax.all_to_all(sending, 'dp', split_axis=0, concat_axis=0, tiled=True)]
    scatter-add x34 -> x0, other arithmetic: 78.8 us -> none  [the longest x16 59.3 us: visit(): near_acc = near_acc.at[picked].add(near_sum)]
    unnamed x1 -> x0, blocking collectives: 64.6 us -> none
    dot_general x48 -> x0, matrix products: 58.5 us -> none  [the longest x16 22.5 us: visit(): jnp.einsum('pie,je->pij', near_blocks, far_block, preferred_element_type=...]
    gather x50 -> x0, local copies, waits for them, and re-layouts: 54.4 us -> none  [the longest x16 32.1 us: visit(): near_blocks = blocks[picked]]
    pallas_call x0 -> x1, Pallas kernels: none -> 54.1 us  [body(): pl.pallas_call(kernel, out_shape=(jax.ShapeDtypeStruct((SHARD, WIDTH), F3...]
    all_to_all x2 -> x0, starting transfers between devices: 17.1 us -> none  [the longest x1 12.5 us: body(): lax.all_to_all(far_mass.astype(jnp.bfloat16), 'dp', split_axis=0, concat_...]
  transfers between devices with their start and end apart: 3 -> 0, of which waited for: 3 -> 0; matrix products, arithmetic and copies ran while one was open for 1% -> 0% of each run, Pallas kernels for 0% -> 0%
where the time goes in v1:
time: 59.5 us; the launch traced here: 59.4 us
  Pallas kernels  54.1 us (91%)
  local copies, waits for them, and re-layouts  4.63 us (8%)
  between operations  0.64 us (1%)
    pallas_call x1, Pallas kernels, body(): pl.pallas_call(kernel, out_shape=(jax.ShapeDtypeStruct((SHARD, WIDTH), F3...  54.1 us
    unnamed x8, local copies, waits for them, and re-layouts  4.12 us

profile of v1, /device:TPU:1, one launch (start us, length us, event | category | flops | bytes accessed | tf_op | source)
XLA Modules:
  0.0 59.4 jit_solution(9284928771477103716)
XLA Ops:
  0.6 0.8 %copy.6.part_hbm = s32[1,1,16,4]{3,2,1,0:T(8,128)S(1)} copy(s32[1,1,16,4]{2,3,1,0:T(4,128)} %param.7) | data formatting | bytes 512 | tf_op args[3]
  1.4 0.0 copy-start
  1.4 1.4 %copy-done = bf16[1024,768]{1,0:T(8,128)(2,1)S(1)} copy-done((bf16[1024,768]{1,0:T(8,128)(2,1)S(1)}, bf16[1024,768]{1,0:T(8,128)(2,1)}, u32[]{:S(2)}) %copy-start) | copy-done | bytes 1572888
  2.8 0.0 copy-start.1
  2.8 0.7 %copy-done.1 = s32[128]{0:T(128)S(1)} copy-done((s32[128]{0:T(128)S(1)}, s32[128]{0:T(128)}, u32[]{:S(2)}) %copy-start.1) | copy-done | bytes 536
  3.5 0.0 copy-start.2
  3.5 0.7 %copy-done.2 = s32[1,1,16]{2,1,0:T(1,128)S(1)} copy-done((s32[1,1,16]{2,1,0:T(1,128)S(1)}, s32[1,1,16]{2,1,0:T(1,128)}, u32[]{:S(2)}) %copy-start.2) | copy-done | bytes 88
  4.1 54.1 %shard_map.59 = (f32[32,768]{1,0:T(8,128)S(1)}, f32[1,128]{1,0:T(1,128)S(1)}) custom-call(bf16[16,2,32,768]{3,2,1,0:T(8,128)(2,1)S(1)} %bitcast.4, s32[1,128]{1,0:T(1,128)S(1)} %bitcast.5, s32[1,1,16]{2,1,0:T(1,128)S(1)} %copy-done.2, s32[1,1,16,4]{3,2,1,0:T(8,128)S(1)} %copy.6.part_hbm), custom_call_target="tpu_custom_call" | custom-call | flops 2415919104 | bytes 4194304 | tf_op jit(solution)/shard_map/pallas_call | solution.py:341
  58.2 0.5 slice_bitcast_fusion
  58.7 0.6 %copy.8 = f32[32,768]{1,0:T(8,128)} copy(f32[32,768]{1,0:T(8,128)S(1)} %get-tuple-element.8) | data formatting | bytes 196608
Async XLA Ops:
  1.4 1.4 %copy-start = (bf16[1024,768]{1,0:T(8,128)(2,1)S(1)}, bf16[1024,768]{1,0:T(8,128)(2,1)}, u32[]{:S(2)}) copy-start(bf16[1024,768]{1,0:T(8,128)(2,1)} %param.4) | copy-start | bytes 4718596
  2.8 0.7 %copy-start.1 = (s32[128]{0:T(128)S(1)}, s32[128]{0:T(128)}, u32[]{:S(2)}) copy-start(s32[128]{0:T(128)} %param.5) | copy-start | bytes 1540
  3.5 0.7 %copy-start.2 = (s32[1,1,16]{2,1,0:T(1,128)S(1)}, s32[1,1,16]{2,1,0:T(1,128)}, u32[]{:S(2)}) copy-start(s32[1,1,16]{2,1,0:T(1,128)} %fetch_hbm.1) | copy-start | bytes 196

commit v2 on v0

v2 whole, which is shorter than its diff:
```python
import jax
import jax.numpy as jnp
from jax import lax
from jax.experimental import pallas as pl
from jax.experimental.pallas import tpu as pltpu
from jax.sharding import PartitionSpec as P

MESH = pl.DeviceIdType.MESH
F32, BF16, I32 = jnp.float32, jnp.bfloat16, jnp.int32

OWNERS, COUNT, DEPTH, WIDTH = 16, 8, 128, 768
SIDE = 4
CHIPS = SIDE * SIDE
SHARD = 32
ROWS = CHIPS * SHARD
PAIR = 2 * SHARD
GROUP = 4
COLS = GROUP * PAIR
FAR = 1e30

KIDS = {0: (2, 1), 2: (5, 3), 5: (8, 7, 4, 6)}
SLOTS = (0, 2, -2, 1, -1, 5, -5, 3, -3, 8, 7, -7, 4, -4, 6, -6)
SLOT = {d: s for s, d in enumerate(SLOTS)}
SLOT[-8] = SLOT[8]
REACH = 3
COUNT_SEM = {2: 0, -2: 1, 5: 2, -5: 3}
EDGES = {}
for parent, kids in KIDS.items():
    for kid in kids:
        for sign in (1, -1):
            EDGES[sign * kid] = sign * parent
EDGE = {d: e for e, d in enumerate(EDGES)}


def below(parent):
    sign = -1 if parent < 0 else 1
    kids = KIDS.get(abs(parent), ())
    if parent == 0:
        return [s * k for k in kids for s in (1, -1)]
    return [sign * k for k in kids]


ORDER = (2, 1, 3, 0)
OFFSETS = [(dx, dy) for dy in ORDER for dx in ORDER]
PEERS = [o for o in OFFSETS if o != (0, 0)]
MATES = [(dx, dy, dc) for dx, dy in OFFSETS for dc in (0, 1) if (dx, dy, dc) != (0, 0, 0)]


def kernel(emb, ints, out_ref, log_ref, xz, cols, kern, acc, mass, ni, cm, tsum, sg, send, recv, loc_sem, sent,
           e_recv, d_recv, c_recv, m_sem, r_recv, a_recv):
    z = lax.axis_index("dp")
    p = lax.axis_index("pair")
    core = lax.rem(p, 2)
    chip = p // 2
    x = lax.rem(chip, SIDE)
    y = chip // SIDE
    half = chip // 2

    def along(d):
        return (lax.rem(z + d + OWNERS, OWNERS), p)

    def place(dx, dy):
        return lax.rem(y + dy, SIDE) * SIDE + lax.rem(x + dx, SIDE)

    def peer(dx, dy):
        return (z, place(dx, dy) * 2 + core)

    other = (z, chip * 2 + 1 - core)

    barrier = pltpu.get_barrier_semaphore()
    for d in range(1, REACH + 1):
        for s in (1, -1):
            pl.semaphore_signal(barrier, 1, device_id=along(s * d), device_id_type=MESH)
    for dx, dy, dc in MATES:
        mate = (z, place(dx, dy) * 2 + lax.rem(core + dc, 2))
        pl.semaphore_signal(barrier, 1, device_id=mate, device_id_type=MESH)

    loads = [
        pltpu.make_async_copy(emb.at[chip, core], cols.at[pl.ds(0, SHARD)], loc_sem.at[0]),
        pltpu.make_async_copy(emb.at[chip, 1 - core], cols.at[pl.ds(SHARD, SHARD)], loc_sem.at[0]),
    ]
    for k in range(CHIPS):
        loads.append(pltpu.make_async_copy(emb.at[k, core], xz.at[pl.ds(k * SHARD, SHARD)], loc_sem.at[1]))
    for c in loads:
        c.start()

    sub8 = lax.broadcasted_iota(I32, (COUNT, 128), 0)
    lane8 = lax.broadcasted_iota(I32, (COUNT, 128), 1)
    sub128 = lax.broadcasted_iota(I32, (128, 128), 0)
    lane128 = lax.broadcasted_iota(I32, (128, 128), 1)
    spread = jnp.where(lane128 // COUNT == sub128, 1.0, 0.0).astype(BF16)
    wide = jnp.dot(ints[...].astype(BF16), spread, preferred_element_type=F32).astype(I32)
    near = sub8 == wide[2:3]
    for k in range(3, 6):
        near = jnp.logical_or(near, sub8 == wide[k:k + 1])
    far = wide[1:2] == lax.rem(lane8, COUNT)
    cm[0] = jnp.where(jnp.logical_and(near, far), 1.0, 0.0)
    pl.semaphore_wait(barrier, 2 * REACH + len(MATES))

    def span(d):
        return (0, 16) if d == 8 else (16, 16) if d == -8 else (0, SHARD)

    def rows_copy(d):
        parent = EDGES[d]
        r0, nr = span(d)
        if parent == 0:
            src = emb.at[chip, core, pl.ds(r0, nr)]
        else:
            src = cols.at[pl.ds(SLOT[parent] * PAIR + r0, nr)]
        return pltpu.make_async_remote_copy(
            src_ref=src, dst_ref=cols.at[pl.ds(SLOT[d] * PAIR + r0, nr)], send_sem=sent.at[0],
            recv_sem=e_recv.at[EDGE[d]], device_id=along(d - parent), device_id_type=MESH)

    def twin_copy(s):
        return pltpu.make_async_remote_copy(
            src_ref=cols.at[pl.ds(s * PAIR, SHARD)], dst_ref=cols.at[pl.ds(s * PAIR + SHARD, SHARD)],
            send_sem=sent.at[1], recv_sem=d_recv.at[s // GROUP], device_id=other, device_id_type=MESH)

    def count_copy(d):
        parent = EDGES[d]
        return pltpu.make_async_remote_copy(
            src_ref=cm.at[SLOT[parent]], dst_ref=cm.at[SLOT[d]], send_sem=sent.at[2],
            recv_sem=c_recv.at[COUNT_SEM.get(d, 4)], device_id=along(d - parent), device_id_type=MESH)

    def rows_in(*ds):
        for d in ds:
            rows_copy(d).wait_recv()
            for k in below(d):
                rows_copy(k).start()
        for d in ds:
            if d != 8:
                twin_copy(SLOT[d]).start()

    def counts_in(*ds):
        for d in ds:
            count_copy(d).wait_recv()
            for k in below(d):
                if k != -8:
                    count_copy(k).start()

    def rest_in():
        come = cm.at[pl.ds(0, OWNERS - 1 - len(COUNT_SEM))]
        pltpu.make_async_copy(come, come, c_recv.at[4]).wait()

    for d in below(0):
        count_copy(d).start()
    for d in below(0):
        rows_copy(d).start()

    pltpu.make_async_copy(xz, xz, loc_sem.at[1]).wait()
    bs = ints[0:1]
    for k in range(ROWS // 128):
        v = xz[k * 128:(k + 1) * 128].astype(F32)
        n = jnp.sum(v * v, axis=1, keepdims=True)
        t = k * 128 + lax.broadcasted_iota(I32, (128, 128), 0)
        lane = lax.broadcasted_iota(I32, (128, 128), 1)
        size = jnp.sum(jnp.where(lane == z * COUNT + t // PAIR, bs, 0.0), axis=1, keepdims=True)
        inside = lax.rem(t // SHARD, 2) * PAIR + core * SHARD + lax.rem(t, SHARD)
        ni[k * 128:(k + 1) * 128] = n + jnp.where(inside.astype(F32) >= size, FAR, 0.0)

    lane1 = lax.broadcasted_iota(I32, (1, 128), 1)
    row64 = lax.broadcasted_iota(I32, (PAIR, 128), 0)
    mine = row64 < SHARD
    inside64 = lax.rem(chip, 2) * PAIR + jnp.where(mine, core * SHARD + row64, (1 - core) * SHARD + row64 - SHARD)
    inside64 = inside64.astype(F32)

    def owner(d):
        return lax.rem(z - d + 2 * OWNERS, OWNERS)

    def far_norms(g):
        parts = []
        for h in range(GROUP // 2):
            two = []
            for s in (g * GROUP + 2 * h, g * GROUP + 2 * h + 1):
                v = cols[s * PAIR:(s + 1) * PAIR].astype(F32)
                n = jnp.sum(v * v, axis=1, keepdims=True)
                block = owner(SLOTS[s]) * COUNT + half
                size = jnp.sum(jnp.where(lane1 == block, bs, 0.0), axis=1, keepdims=True)
                two.append(n + jnp.where(inside64 >= size, FAR, 0.0))
            n = jnp.concatenate(two, axis=0)
            parts.append(jnp.sum(jnp.where(sub128 == lane128, n, 0.0), axis=0, keepdims=True))
        return jnp.concatenate(parts, axis=1)

    def near(g):
        if g == 0:
            both = cols.at[pl.ds(0, PAIR)]
            pltpu.make_async_copy(both, both, loc_sem.at[0]).wait()
        come = cols.at[pl.ds(0, (GROUP - (g == 0)) * SHARD)]
        pltpu.make_async_copy(come, come, d_recv.at[g]).wait()
        nj = far_norms(g)
        for r in range(0, ROWS, 256):
            dots = lax.dot_general(xz[r:r + 256], cols[g * COLS:(g + 1) * COLS], (((1,), (1,)), ((), ())),
                                   preferred_element_type=F32)
            n = ni[r:r + 256]
            dist = jnp.concatenate([n, n], axis=1) + nj - 2.0 * dots
            kern[r:r + 256, g * COLS:(g + 1) * COLS] = jnp.exp(-dist)

    counts_in(2, -2)
    rows_in(2, -2)
    rows_in(1, -1)
    counts_in(5, -5)
    rows_in(5, -5)
    rows_in(3, -3)
    rest_in()

    slot1 = lane1 // COUNT
    own1 = jnp.zeros((1, 128), I32)
    for s, d in enumerate(SLOTS):
        own1 = jnp.where(slot1 == s, owner(d), own1)
    own1 = own1 * COUNT + lax.rem(lane1, COUNT)
    perm = jnp.where(sub128 == own1, 1.0, 0.0).astype(BF16)
    pick = jnp.where(lane8 == z * COUNT + sub8, 1.0, 0.0).astype(BF16)
    there = cm[...].reshape(OWNERS * COUNT, 128).astype(BF16)
    pairs = jnp.dot(cm[0].astype(BF16), perm, preferred_element_type=F32) + lax.dot_general(
        pick, there, (((1,), (1,)), ((), ())), preferred_element_type=F32)
    tsum[2 * CHIPS - 1] = pairs
    for i, (dx, dy, dc) in enumerate(MATES):
        pltpu.make_async_remote_copy(
            src_ref=tsum.at[2 * CHIPS - 1], dst_ref=tsum.at[i], send_sem=m_sem.at[0], recv_sem=m_sem.at[1],
            device_id=(z, place(dx, dy) * 2 + lax.rem(core + dc, 2)), device_id_type=MESH).start()
    near(0)
    near(1)
    rows_in(8, -8)
    rows_in(7, -7)
    rows_in(4, -4)
    rows_in(6, -6)
    near(2)
    near(3)
    mates = tsum.at[pl.ds(0, len(MATES))]
    pltpu.make_async_copy(mates, mates, m_sem.at[1]).wait()
    total = tsum[2 * CHIPS - 1]
    for i in range(len(MATES)):
        total = total + tsum[i]
    for s in range(0, OWNERS, 2):
        two = [jnp.sum(jnp.where(lane8 == t * COUNT + half, total, 0.0), axis=1, keepdims=True) for t in (s, s + 1)]
        sg[:, s * PAIR:(s + 2) * PAIR] = jnp.where(lane8 < PAIR, two[0], two[1])

    def sums(row, c0, c1):
        k = kern[pl.ds(row * 128, 128), c0:c1]
        s0 = jnp.broadcast_to(sg[pl.ds(row * 2, 1), c0:c1], (PAIR, c1 - c0))
        s1 = jnp.broadcast_to(sg[pl.ds(row * 2 + 1, 1), c0:c1], (PAIR, c1 - c0))
        s = jnp.concatenate([s0, s1], axis=0)
        w = s * k.astype(BF16).astype(F32)
        hi = w.astype(BF16)
        lo = (w - hi.astype(F32)).astype(BF16)
        far = cols[c0:c1]
        t = jnp.dot(hi, far, preferred_element_type=F32) + jnp.dot(lo, far, preferred_element_type=F32)
        m = s * k
        return t, sum(m[:, 128 * h:128 * (h + 1)] for h in range((c1 - c0) // 128))

    lane32 = lax.broadcasted_iota(I32, (SHARD, 128), 1)
    sub32 = lax.broadcasted_iota(I32, (SHARD, 128), 0)
    i = 0
    for dy in ORDER:
        row = lax.rem(y + dy, SIDE)
        r = pl.ds(row * 128, 128)
        t, m = sums(row, 0, 4 * COLS)
        m = jnp.sum(m, axis=1, keepdims=True)
        mass[dy] = jnp.sum(jnp.where(sub128 == lane128, m, 0.0), axis=0, keepdims=True)
        acc[r] = t
        for dx in ORDER:
            if (dx, dy) == (0, 0):
                continue
            send[i] = acc[pl.ds(place(dx, dy) * SHARD, SHARD)].astype(BF16)
            pltpu.make_async_remote_copy(
                src_ref=send.at[i], dst_ref=recv.at[i], send_sem=sent.at[3], recv_sem=r_recv.at[ORDER.index(dy)],
                device_id=peer(dx, dy), device_id_type=MESH).start()
            pltpu.make_async_remote_copy(
                src_ref=mass.at[dy], dst_ref=mass.at[SIDE + i], send_sem=sent.at[4], recv_sem=a_recv.at[0],
                device_id=peer(dx, dy), device_id_type=MESH).start()
            i += 1

    v = acc[pl.ds(chip * SHARD, SHARD)]
    a = mass[0]
    for h in range(SIDE):
        come = pl.ds(h * SIDE, SIDE - (h == SIDE - 1))
        pltpu.make_async_copy(recv.at[come], recv.at[come], r_recv.at[h]).wait()
        for i in range(h * SIDE, min((h + 1) * SIDE, len(PEERS))):
            v = v + recv[i].astype(F32)
    come = mass.at[pl.ds(SIDE, len(PEERS))]
    pltpu.make_async_copy(come, come, a_recv.at[0]).wait()
    for i in range(len(PEERS)):
        a = a + mass[SIDE + i]
    out_ref[...] = v
    m = jnp.sum(jnp.where(lane32 == x * SHARD + sub32, a, 0.0), axis=1, keepdims=True)
    m = jnp.log(1.0 + m)
    log_ref[...] = jnp.sum(jnp.where(sub32 == lane32, m, 0.0), axis=0, keepdims=True)
    shards = cols.at[pl.ds(0, (OWNERS - 1) * SHARD)]
    counted = cm.at[pl.ds(0, OWNERS - 1)]
    for what, sem in ((shards, sent.at[0]), (shards, sent.at[1]), (counted, sent.at[2]), (send, sent.at[3]),
                      (come, sent.at[4]), (mates, m_sem.at[0])):
        pltpu.make_async_copy(what, what, sem).wait()


def body(embeddings, block_sizes, fetch_blocks, partners):
    hbm = pl.BlockSpec(memory_space=pltpu.HBM)
    vmem = pl.BlockSpec(memory_space=pltpu.VMEM)
    dma = pltpu.SemaphoreType.DMA
    edges = len(EDGES)
    room = ((0, 0), (0, 128 - OWNERS))
    ints = jnp.concatenate([
        block_sizes.reshape(1, 128),
        jnp.pad(fetch_blocks.reshape(1, OWNERS), room),
        jnp.pad(jnp.swapaxes(partners, 2, 3).reshape(4, OWNERS), room),
        jnp.zeros((2, 128), I32),
    ]).astype(F32)
    out, logs = pl.pallas_call(
        kernel,
        out_shape=(jax.ShapeDtypeStruct((SHARD, WIDTH), F32), jax.ShapeDtypeStruct((1, 128), F32)),
        in_specs=[hbm, vmem],
        out_specs=(vmem, vmem),
        scratch_shapes=[
            pltpu.VMEM((ROWS, WIDTH), BF16),
            pltpu.VMEM((OWNERS * PAIR, WIDTH), BF16),
            pltpu.VMEM((ROWS, OWNERS * PAIR), F32),
            pltpu.VMEM((ROWS, WIDTH), F32),
            pltpu.VMEM((SIDE + len(PEERS), 1, 128), F32),
            pltpu.VMEM((ROWS, 128), F32),
            pltpu.VMEM((OWNERS, COUNT, 128), F32),
            pltpu.VMEM((2 * CHIPS, COUNT, 128), F32),
            pltpu.VMEM((COUNT, OWNERS * PAIR), F32),
            pltpu.VMEM((len(PEERS), SHARD, WIDTH), BF16),
            pltpu.VMEM((len(PEERS), SHARD, WIDTH), BF16),
            dma((2,)),
            dma((5,)),
            dma((edges,)),
            dma((OWNERS // GROUP,)),
            dma((len(COUNT_SEM) + 1,)),
            dma((2,)),
            dma((SIDE,)),
            dma((1,)),
        ],
        compiler_params=pltpu.CompilerParams(collective_id=0, has_side_effects=True, vmem_limit_bytes=53 << 20),
        cost_estimate=pl.CostEstimate(flops=3 * 2 * 512 * 1024 * 768, bytes_accessed=4 << 20, transcendentals=512 * 1024),
    )(embeddings.reshape(CHIPS, 2, SHARD, WIDTH), ints)
    return out, logs[0, :SHARD]


def solution(mesh):
    return jax.shard_map(
        body,
        mesh=mesh,
        in_specs=(P("dp", None), P(), P("dp", "pair", None), P("dp", "pair", None, None)),
        out_specs=(P(("dp", "pair"), None), P(("dp", "pair"))),
        check_vma=False,
    )
```

time: 639 us -> 50.5 us (0.08)
  blocking collectives: 238 us -> 0 us
  waiting for transfers between devices: 157 us -> 0 us
  other arithmetic: 87.8 us -> 0.77 us
  local copies, waits for them, and re-layouts: 61.6 us -> 1.23 us
  matrix products: 58.5 us -> 0 us
  Pallas kernels: 0 us -> 47.7 us
  starting transfers between devices: 17.2 us -> 0 us
  between operations: 14.8 us -> 0.65 us
    all_to_all x2 -> x0, blocking collectives: 174 us -> none  [the longest x1 147 us: body(): lax.all_to_all(far_sums.astype(jnp.bfloat16), 'dp', split_axis=0, concat_...]
    all_to_all x2 -> x0, waiting for transfers between devices: 143 us -> none  [the longest x1 134 us: body(): lax.all_to_all(sending, 'dp', split_axis=0, concat_axis=0, tiled=True)]
    scatter-add x34 -> x0, other arithmetic: 78.8 us -> none  [the longest x16 59.3 us: visit(): near_acc = near_acc.at[picked].add(near_sum)]
    unnamed x1 -> x0, blocking collectives: 64.6 us -> none
    dot_general x48 -> x0, matrix products: 58.5 us -> none  [the longest x16 22.5 us: visit(): jnp.einsum('pie,je->pij', near_blocks, far_block, preferred_element_type=...]
    gather x50 -> x0, local copies, waits for them, and re-layouts: 54.4 us -> none  [the longest x16 32.1 us: visit(): near_blocks = blocks[picked]]
    pallas_call x0 -> x1, Pallas kernels: none -> 47.7 us  [body(): pl.pallas_call(kernel, out_shape=(jax.ShapeDtypeStruct((SHARD, WIDTH), F3...]
    all_to_all x2 -> x0, starting transfers between devices: 17.1 us -> none  [the longest x1 12.5 us: body(): lax.all_to_all(far_mass.astype(jnp.bfloat16), 'dp', split_axis=0, concat_...]
  transfers between devices with their start and end apart: 3 -> 0, of which waited for: 3 -> 0; matrix products, arithmetic and copies ran while one was open for 1% -> 0% of each run, Pallas kernels for 0% -> 0%
where the time goes in v2:
time: 50.5 us; the launch traced here: 50.3 us
  Pallas kernels  47.7 us (94%)
  local copies, waits for them, and re-layouts  1.23 us (2%)
  other arithmetic  0.77 us (2%)
  between operations  0.65 us (1%)
    pallas_call x1, Pallas kernels, body(): pl.pallas_call(kernel, out_shape=(jax.ShapeDtypeStruct((SHARD, WIDTH), F3...  47.7 us

profile of v2, /device:TPU:1, one launch (start us, length us, event | category | flops | bytes accessed | tf_op | source)
XLA Modules:
  0.0 50.3 jit_solution(5263301302151210830)
XLA Ops:
  0.6 0.1 pad.13.clone
  0.7 0.8 %fusion.1.ints = f32[8,128]{1,0:T(8,128)S(1)} fusion(s32[4,16]{1,0:T(4,128)} %bitcast.8, s32[1,16]{1,0:T(1,128)} %bitcast.9, s32[1,128]{1,0:T(1,128)} %bitcast.10, s32[8]{0:T(128)S(1)} %pad.13.clone), kind=kLoop, calls=%fused_computation.2 | loop fusion | flops 4096 | bytes 4960 | tf_op jit(solution)/shard_map/convert_element_type | solution.py:306
  1.5 47.7 %shard_map.59 = (f32[32,768]{1,0:T(8,128)S(1)}, f32[1,128]{1,0:T(1,128)S(1)}) custom-call(bf16[16,2,32,768]{3,2,1,0:T(8,128)(2,1)} %bitcast.11, f32[8,128]{1,0:T(8,128)S(1)} %fusion.1.ints), custom_call_target="tpu_custom_call" | custom-call | flops 2415919104 | bytes 4194304 | tf_op jit(solution)/shard_map/pallas_call | solution.py:307
  49.2 0.5 %slice_bitcast_fusion = f32[32]{0:T(128)} fusion(f32[1,128]{1,0:T(1,128)S(1)} %get-tuple-element.5), kind=kLoop, calls=%fused_computation.4 | loop fusion | bytes 256 | tf_op jit(solution)/shard_map/squeeze | solution.py:336
  49.7 0.6 %copy.7 = f32[32,768]{1,0:T(8,128)} copy(f32[32,768]{1,0:T(8,128)S(1)} %get-tuple-element.8) | data formatting | bytes 196608
  (1 shorter events, 0.0 us)

commit v3 on v2

--- a/solution.py
+++ b/solution.py
@@ -15,6 +15,7 @@
 ROWS = CHIPS * SHARD
 PAIR = 2 * SHARD
 GROUP = 4
+CUT = 512
 COLS = GROUP * PAIR
 FAR = 1e30
 
@@ -22,6 +23,8 @@
 SLOTS = (0, 2, -2, 1, -1, 5, -5, 3, -3, 8, 7, -7, 4, -4, 6, -6)
 SLOT = {d: s for s, d in enumerate(SLOTS)}
 SLOT[-8] = SLOT[8]
+UNITS = [(s, side) for s in range(8) for side in (0, 1)] + [(s, side) for side in (0, 1) for s in range(8, 16)]
+UNIT = {unit: u for u, unit in enumerate(UNITS)}
 REACH = 3
 COUNT_SEM = {2: 0, -2: 1, 5: 2, -5: 3}
 EDGES = {}
@@ -41,12 +44,14 @@
 
 
 ORDER = (2, 1, 3, 0)
+HOPS = (2, 1, 3)
 OFFSETS = [(dx, dy) for dy in ORDER for dx in ORDER]
 PEERS = [o for o in OFFSETS if o != (0, 0)]
 MATES = [(dx, dy, dc) for dx, dy in OFFSETS for dc in (0, 1) if (dx, dy, dc) != (0, 0, 0)]
 
 
-def kernel(emb, ints, out_ref, log_ref, xz, cols, kern, acc, mass, ni, cm, tsum, sg, send, recv, loc_sem, sent,
+def kernel(emb, ints, out_ref, log_ref, xz, cols, kern, acc, fold, mass, ni, cm, tsum, sg, send_x, recv_x, send_y, recv_y,
+           sum_y, last_x, last_y, loc_sem, sent,
            e_recv, d_recv, c_recv, m_sem, r_recv, a_recv):
     z = lax.axis_index("dp")
     p = lax.axis_index("pair")
@@ -100,21 +105,24 @@
     def span(d):
         return (0, 16) if d == 8 else (16, 16) if d == -8 else (0, SHARD)
 
+    def held(s, side, r0=0, nr=SHARD):
+        return cols.at[pl.ds(UNIT[s, side] * SHARD + r0, nr)]
+
     def rows_copy(d):
         parent = EDGES[d]
         r0, nr = span(d)
         if parent == 0:
             src = emb.at[chip, core, pl.ds(r0, nr)]
         else:
-            src = cols.at[pl.ds(SLOT[parent] * PAIR + r0, nr)]
+            src = held(SLOT[parent], 0, r0, nr)
         return pltpu.make_async_remote_copy(
-            src_ref=src, dst_ref=cols.at[pl.ds(SLOT[d] * PAIR + r0, nr)], send_sem=sent.at[0],
+            src_ref=src, dst_ref=held(SLOT[d], 0, r0, nr), send_sem=sent.at[0],
             recv_sem=e_recv.at[EDGE[d]], device_id=along(d - parent), device_id_type=MESH)
 
     def twin_copy(s):
         return pltpu.make_async_remote_copy(
-            src_ref=cols.at[pl.ds(s * PAIR, SHARD)], dst_ref=cols.at[pl.ds(s * PAIR + SHARD, SHARD)],
-            send_sem=sent.at[1], recv_sem=d_recv.at[s // GROUP], device_id=other, device_id_type=MESH)
+            src_ref=held(s, 0), dst_ref=held(s, 1),
+            send_sem=sent.at[1], recv_sem=d_recv.at[min(s // GROUP, 2)], device_id=other, device_id_type=MESH)
 
     def count_copy(d):
         parent = EDGES[d]
@@ -159,25 +167,24 @@
         ni[k * 128:(k + 1) * 128] = n + jnp.where(inside.astype(F32) >= size, FAR, 0.0)
 
     lane1 = lax.broadcasted_iota(I32, (1, 128), 1)
-    row64 = lax.broadcasted_iota(I32, (PAIR, 128), 0)
-    mine = row64 < SHARD
-    inside64 = lax.rem(chip, 2) * PAIR + jnp.where(mine, core * SHARD + row64, (1 - core) * SHARD + row64 - SHARD)
-    inside64 = inside64.astype(F32)
+    row32 = lax.broadcasted_iota(I32, (SHARD, 128), 0)
+    inside32 = [(lax.rem(chip, 2) * PAIR + c * SHARD + row32).astype(F32) for c in (core, 1 - core)]
 
     def owner(d):
         return lax.rem(z - d + 2 * OWNERS, OWNERS)
 
     def far_norms(g):
         parts = []
-        for h in range(GROUP // 2):
-            two = []
-            for s in (g * GROUP + 2 * h, g * GROUP + 2 * h + 1):
-                v = cols[s * PAIR:(s + 1) * PAIR].astype(F32)
+        for u0 in range(g * 8, g * 8 + 8, 4):
+            units = []
+            for u in range(u0, u0 + 4):
+                s, side = UNITS[u]
+                v = cols[u * SHARD:(u + 1) * SHARD].astype(F32)
                 n = jnp.sum(v * v, axis=1, keepdims=True)
                 block = owner(SLOTS[s]) * COUNT + half
                 size = jnp.sum(jnp.where(lane1 == block, bs, 0.0), axis=1, keepdims=True)
-                two.append(n + jnp.where(inside64 >= size, FAR, 0.0))
-            n = jnp.concatenate(two, axis=0)
+                units.append(n + jnp.where(inside32[side] >= size, FAR, 0.0))
+            n = jnp.concatenate(units, axis=0)
             parts.append(jnp.sum(jnp.where(sub128 == lane128, n, 0.0), axis=0, keepdims=True))
         return jnp.concatenate(parts, axis=1)
 
@@ -185,8 +192,9 @@
         if g == 0:
             both = cols.at[pl.ds(0, PAIR)]
             pltpu.make_async_copy(both, both, loc_sem.at[0]).wait()
-        come = cols.at[pl.ds(0, (GROUP - (g == 0)) * SHARD)]
-        pltpu.make_async_copy(come, come, d_recv.at[g]).wait()
+        if g != 2:
+            come = cols.at[pl.ds(0, (GROUP - 1, GROUP, 0, 2 * GROUP)[g] * SHARD)]
+            pltpu.make_async_copy(come, come, d_recv.at[min(g, 2)]).wait()
         nj = far_norms(g)
         for r in range(0, ROWS, 256):
             dots = lax.dot_general(xz[r:r + 256], cols[g * COLS:(g + 1) * COLS], (((1,), (1,)), ((), ())),
@@ -225,15 +233,17 @@
     rows_in(4, -4)
     rows_in(6, -6)
     near(2)
-    near(3)
     mates = tsum.at[pl.ds(0, len(MATES))]
     pltpu.make_async_copy(mates, mates, m_sem.at[1]).wait()
     total = tsum[2 * CHIPS - 1]
     for i in range(len(MATES)):
         total = total + tsum[i]
-    for s in range(0, OWNERS, 2):
-        two = [jnp.sum(jnp.where(lane8 == t * COUNT + half, total, 0.0), axis=1, keepdims=True) for t in (s, s + 1)]
-        sg[:, s * PAIR:(s + 2) * PAIR] = jnp.where(lane8 < PAIR, two[0], two[1])
+    times = [jnp.sum(jnp.where(lane8 == s * COUNT + half, total, 0.0), axis=1, keepdims=True) for s in range(OWNERS)]
+    for u in range(0, 2 * OWNERS, 4):
+        four = [times[UNITS[u + k][0]] for k in range(4)]
+        low = jnp.where(lane8 < SHARD, four[0], four[1])
+        high = jnp.where(lane8 < 3 * SHARD, four[2], four[3])
+        sg[:, u * SHARD:(u + 4) * SHARD] = jnp.where(lane8 < PAIR, low, high)
 
     def sums(row, c0, c1):
         k = kern[pl.ds(row * 128, 128), c0:c1]
@@ -248,48 +258,91 @@
         m = s * k
         return t, sum(m[:, 128 * h:128 * (h + 1)] for h in range((c1 - c0) // 128))
 
+    acc[ORDER[0]], fold[...] = sums(lax.rem(y + ORDER[0], SIDE), 0, 3 * COLS)
+    near(3)
+
     lane32 = lax.broadcasted_iota(I32, (SHARD, 128), 1)
     sub32 = lax.broadcasted_iota(I32, (SHARD, 128), 0)
+
+    def spot(step):
+        return pl.ds(lax.rem(x + step, SIDE) * SHARD, SHARD)
+
+    def send_to(src, dst, sem, dx, dy, kind):
+        pltpu.make_async_remote_copy(src_ref=src, dst_ref=dst, send_sem=sent.at[kind], recv_sem=sem,
+                                     device_id=peer(dx, dy), device_id_type=MESH).start()
+
     i = 0
     for dy in ORDER:
-        row = lax.rem(y + dy, SIDE)
-        r = pl.ds(row * 128, 128)
-        t, m = sums(row, 0, 4 * COLS)
+        if dy == ORDER[0]:
+            t, m = sums(lax.rem(y + dy, SIDE), 3 * COLS, 4 * COLS)
+            t, m = t + acc[dy], m + fold[...]
+        else:
+            t, m = sums(lax.rem(y + dy, SIDE), 0, 4 * COLS)
+        acc[dy] = t
+        if dy:
+            send_y[dy - 1] = t[:, CUT:].astype(BF16)
+            send_to(send_y.at[dy - 1], recv_y.at[dy - 1], r_recv.at[4], 0, dy, 4)
+        for dx in HOPS:
+            send_x[dx - 1, dy] = acc[dy, spot(dx), :CUT].astype(BF16)
+            send_to(send_x.at[dx - 1, dy], recv_x.at[dx - 1, dy], r_recv.at[dy], dx, 0, 3)
         m = jnp.sum(m, axis=1, keepdims=True)
         mass[dy] = jnp.sum(jnp.where(sub128 == lane128, m, 0.0), axis=0, keepdims=True)
-        acc[r] = t
         for dx in ORDER:
-            if (dx, dy) == (0, 0):
-                continue
-            send[i] = acc[pl.ds(place(dx, dy) * SHARD, SHARD)].astype(BF16)
-            pltpu.make_async_remote_copy(
-                src_ref=send.at[i], dst_ref=recv.at[i], send_sem=sent.at[3], recv_sem=r_recv.at[ORDER.index(dy)],
-                device_id=peer(dx, dy), device_id_type=MESH).start()
-            pltpu.make_async_remote_copy(
-                src_ref=mass.at[dy], dst_ref=mass.at[SIDE + i], send_sem=sent.at[4], recv_sem=a_recv.at[0],
-                device_id=peer(dx, dy), device_id_type=MESH).start()
-            i += 1
-
-    v = acc[pl.ds(chip * SHARD, SHARD)]
+            if (dx, dy) != (0, 0):
+                send_to(mass.at[dy], mass.at[SIDE + i], a_recv.at[0], dx, dy, 5)
+                i += 1
+
+    def come(ref, sem):
+        pltpu.make_async_copy(ref, ref, sem).wait()
+
+    def first_x(dy):
+        come(recv_x.at[:, dy], r_recv.at[dy])
+        v = acc[dy, spot(0), :CUT]
+        for k in range(SIDE - 1):
+            v = v + recv_x[k, dy].astype(F32)
+        return v
+
+    def along_y(dy):
+        last_y[dy - 1] = first_x(dy)
+        send_to(last_y.at[dy - 1], last_y.at[SIDE - 2 + dy], r_recv.at[6], 0, dy, 7)
+
+    along_y(2)
+    along_y(1)
+    come(recv_y, r_recv.at[4])
+    v = acc[0, :, CUT:]
+    for k in range(SIDE - 1):
+        v = v + recv_y[k].astype(F32)
+    sum_y[...] = v
+    for dx in HOPS:
+        last_x[dx - 1] = sum_y[spot(dx)]
+        send_to(last_x.at[dx - 1], last_x.at[SIDE - 2 + dx], r_recv.at[5], dx, 0, 6)
+    along_y(3)
+    v = first_x(0)
     a = mass[0]
-    for h in range(SIDE):
-        come = pl.ds(h * SIDE, SIDE - (h == SIDE - 1))
-        pltpu.make_async_copy(recv.at[come], recv.at[come], r_recv.at[h]).wait()
-        for i in range(h * SIDE, min((h + 1) * SIDE, len(PEERS))):
-            v = v + recv[i].astype(F32)
-    come = mass.at[pl.ds(SIDE, len(PEERS))]
-    pltpu.make_async_copy(come, come, a_recv.at[0]).wait()
-    for i in range(len(PEERS)):
-        a = a + mass[SIDE + i]
-    out_ref[...] = v
+    got = mass.at[pl.ds(SIDE, len(PEERS))]
+    come(got, a_recv.at[0])
+    for k in range(len(PEERS)):
+        a = a + mass[SIDE + k]
     m = jnp.sum(jnp.where(lane32 == x * SHARD + sub32, a, 0.0), axis=1, keepdims=True)
     m = jnp.log(1.0 + m)
     log_ref[...] = jnp.sum(jnp.where(sub32 == lane32, m, 0.0), axis=0, keepdims=True)
+    w = sum_y[spot(0)]
+    there_x = last_x.at[pl.ds(SIDE - 1, SIDE - 1)]
+    there_y = last_y.at[pl.ds(SIDE - 1, SIDE - 1)]
+    come(there_x, r_recv.at[5])
+    for k in range(SIDE - 1):
+        w = w + last_x[SIDE - 1 + k]
+    out_ref[:, CUT:] = w
+    come(there_y, r_recv.at[6])
+    for k in range(SIDE - 1):
+        v = v + last_y[SIDE - 1 + k]
+    out_ref[:, :CUT] = v
     shards = cols.at[pl.ds(0, (OWNERS - 1) * SHARD)]
     counted = cm.at[pl.ds(0, OWNERS - 1)]
-    for what, sem in ((shards, sent.at[0]), (shards, sent.at[1]), (counted, sent.at[2]), (send, sent.at[3]),
-                      (come, sent.at[4]), (mates, m_sem.at[0])):
-        pltpu.make_async_copy(what, what, sem).wait()
+    for what, sem in ((shards, sent.at[0]), (shards, sent.at[1]), (counted, sent.at[2]), (recv_x, sent.at[3]),
+                      (recv_y, sent.at[4]), (got, sent.at[5]), (there_x, sent.at[6]), (there_y, sent.at[7]),
+                      (mates, m_sem.at[0])):
+        come(what, sem)
 
 
 def body(embeddings, block_sizes, fetch_blocks, partners):
@@ -313,21 +366,27 @@
             pltpu.VMEM((ROWS, WIDTH), BF16),
             pltpu.VMEM((OWNERS * PAIR, WIDTH), BF16),
             pltpu.VMEM((ROWS, OWNERS * PAIR), F32),
-            pltpu.VMEM((ROWS, WIDTH), F32),
+            pltpu.VMEM((SIDE, 128, WIDTH), F32),
+            pltpu.VMEM((128, 128), F32),
             pltpu.VMEM((SIDE + len(PEERS), 1, 128), F32),
             pltpu.VMEM((ROWS, 128), F32),
             pltpu.VMEM((OWNERS, COUNT, 128), F32),
             pltpu.VMEM((2 * CHIPS, COUNT, 128), F32),
             pltpu.VMEM((COUNT, OWNERS * PAIR), F32),
-            pltpu.VMEM((len(PEERS), SHARD, WIDTH), BF16),
-            pltpu.VMEM((len(PEERS), SHARD, WIDTH), BF16),
+            pltpu.VMEM((SIDE - 1, SIDE, SHARD, CUT), BF16),
+            pltpu.VMEM((SIDE - 1, SIDE, SHARD, CUT), BF16),
+            pltpu.VMEM((SIDE - 1, 128, WIDTH - CUT), BF16),
+            pltpu.VMEM((SIDE - 1, 128, WIDTH - CUT), BF16),
+            pltpu.VMEM((128, WIDTH - CUT), F32),
+            pltpu.VMEM((2 * (SIDE - 1), SHARD, WIDTH - CUT), F32),
+            pltpu.VMEM((2 * (SIDE - 1), SHARD, CUT), F32),
             dma((2,)),
-            dma((5,)),
+            dma((8,)),
             dma((edges,)),
-            dma((OWNERS // GROUP,)),
+            dma((3,)),
             dma((len(COUNT_SEM) + 1,)),
             dma((2,)),
-            dma((SIDE,)),
+            dma((7,)),
             dma((1,)),
         ],
         compiler_params=pltpu.CompilerParams(collective_id=0, has_side_effects=True, vmem_limit_bytes=53 << 20),

time: 50.5 us -> 47.6 us (0.943)
  Pallas kernels: 47.7 us -> 44.8 us
    pallas_call x1, Pallas kernels: 47.7 us -> 44.8 us  [body(): pl.pallas_call(kernel, out_shape=(jax.ShapeDtypeStruct((SHARD, WIDTH), F3...]
where the time goes in v3:
time: 47.6 us; the launch traced here: 47.5 us
  Pallas kernels  44.8 us (94%)
  local copies, waits for them, and re-layouts  1.23 us (3%)
  other arithmetic  0.77 us (2%)
  between operations  0.65 us (1%)
    pallas_call x1, Pallas kernels, body(): pl.pallas_call(kernel, out_shape=(jax.ShapeDtypeStruct((SHARD, WIDTH), F3...  44.8 us

profile of v3, /device:TPU:1, one launch (start us, length us, event | category | flops | bytes accessed | tf_op | source)
XLA Modules:
  0.0 47.5 jit_solution(16354098405307133634)
XLA Ops:
  0.6 0.1 pad.13.clone
  0.7 0.8 %fusion.1.ints = f32[8,128]{1,0:T(8,128)S(1)} fusion(s32[4,16]{1,0:T(4,128)} %bitcast.8, s32[1,16]{1,0:T(1,128)} %bitcast.9, s32[1,128]{1,0:T(1,128)} %bitcast.10, s32[8]{0:T(128)S(1)} %pad.13.clone), kind=kLoop, calls=%fused_computation.2 | loop fusion | flops 4096 | bytes 4960 | tf_op jit(solution)/shard_map/convert_element_type | solution.py:359
  1.5 44.8 %shard_map.59 = (f32[32,768]{1,0:T(8,128)S(1)}, f32[1,128]{1,0:T(1,128)S(1)}) custom-call(bf16[16,2,32,768]{3,2,1,0:T(8,128)(2,1)} %bitcast.11, f32[8,128]{1,0:T(8,128)S(1)} %fusion.1.ints), custom_call_target="tpu_custom_call" | custom-call | flops 2415919104 | bytes 4194304 | tf_op jit(solution)/shard_map/pallas_call | solution.py:360
  46.3 0.5 %slice_bitcast_fusion = f32[32]{0:T(128)} fusion(f32[1,128]{1,0:T(1,128)S(1)} %get-tuple-element.5), kind=kLoop, calls=%fused_computation.4 | loop fusion | bytes 256 | tf_op jit(solution)/shard_map/squeeze | solution.py:395
  46.8 0.6 %copy.7 = f32[32,768]{1,0:T(8,128)} copy(f32[32,768]{1,0:T(8,128)S(1)} %get-tuple-element.8) | data formatting | bytes 196608
  (1 shorter events, 0.0 us)

commit v4 on v3

--- a/solution.py
+++ b/solution.py
@@ -15,7 +15,7 @@
 ROWS = CHIPS * SHARD
 PAIR = 2 * SHARD
 GROUP = 4
-CUT = 512
+CUT = 640
 COLS = GROUP * PAIR
 FAR = 1e30
 
@@ -50,8 +50,8 @@
 MATES = [(dx, dy, dc) for dx, dy in OFFSETS for dc in (0, 1) if (dx, dy, dc) != (0, 0, 0)]
 
 
-def kernel(emb, ints, out_ref, log_ref, xz, cols, kern, acc, fold, mass, ni, cm, tsum, sg, send_x, recv_x, send_y, recv_y,
-           sum_y, last_x, last_y, loc_sem, sent,
+def kernel(emb, ints, out_ref, log_ref, xz, cols, kern, acc, fold, mass, ni, cm, tsum, sg, send_u, recv_u, send_v, recv_v,
+           sum_v, last_u, last_v, loc_sem, sent,
            e_recv, d_recv, c_recv, m_sem, r_recv, a_recv):
     z = lax.axis_index("dp")
     p = lax.axis_index("pair")
@@ -67,8 +67,11 @@
     def place(dx, dy):
         return lax.rem(y + dy, SIDE) * SIDE + lax.rem(x + dx, SIDE)
 
-    def peer(dx, dy):
-        return (z, place(dx, dy) * 2 + core)
+    own_u = x + core * (y - x)
+    own_v = y + core * (x - y)
+
+    def peer(du, dv):
+        return (z, place(du + core * (dv - du), dv + core * (du - dv)) * 2 + core)
 
     other = (z, chip * 2 + 1 - core)
 
@@ -85,7 +88,8 @@
         pltpu.make_async_copy(emb.at[chip, 1 - core], cols.at[pl.ds(SHARD, SHARD)], loc_sem.at[0]),
     ]
     for k in range(CHIPS):
-        loads.append(pltpu.make_async_copy(emb.at[k, core], xz.at[pl.ds(k * SHARD, SHARD)], loc_sem.at[1]))
+        other_way = k % SIDE * SIDE + k // SIDE
+        loads.append(pltpu.make_async_copy(emb.at[k + core * (other_way - k), core], xz.at[pl.ds(k * SHARD, SHARD)], loc_sem.at[1]))
     for c in loads:
         c.start()
 
@@ -160,10 +164,11 @@
     for k in range(ROWS // 128):
         v = xz[k * 128:(k + 1) * 128].astype(F32)
         n = jnp.sum(v * v, axis=1, keepdims=True)
-        t = k * 128 + lax.broadcasted_iota(I32, (128, 128), 0)
+        at = k * SIDE + sub128 // SHARD
+        at = at + core * (lax.rem(at, SIDE) * SIDE + at // SIDE - at)
         lane = lax.broadcasted_iota(I32, (128, 128), 1)
-        size = jnp.sum(jnp.where(lane == z * COUNT + t // PAIR, bs, 0.0), axis=1, keepdims=True)
-        inside = lax.rem(t // SHARD, 2) * PAIR + core * SHARD + lax.rem(t, SHARD)
+        size = jnp.sum(jnp.where(lane == z * COUNT + at // 2, bs, 0.0), axis=1, keepdims=True)
+        inside = lax.rem(at, 2) * PAIR + core * SHARD + lax.rem(sub128, SHARD)
         ni[k * 128:(k + 1) * 128] = n + jnp.where(inside.astype(F32) >= size, FAR, 0.0)
 
     lane1 = lax.broadcasted_iota(I32, (1, 128), 1)
@@ -247,9 +252,11 @@
 
     def sums(row, c0, c1):
         k = kern[pl.ds(row * 128, 128), c0:c1]
-        s0 = jnp.broadcast_to(sg[pl.ds(row * 2, 1), c0:c1], (PAIR, c1 - c0))
-        s1 = jnp.broadcast_to(sg[pl.ds(row * 2 + 1, 1), c0:c1], (PAIR, c1 - c0))
-        s = jnp.concatenate([s0, s1], axis=0)
+        s = []
+        for h in range(SIDE):
+            block = (row * SIDE + h + core * (h * SIDE + row - row * SIDE - h)) // 2
+            s.append(jnp.broadcast_to(sg[pl.ds(block, 1), c0:c1], (SHARD, c1 - c0)))
+        s = jnp.concatenate(s, axis=0)
         w = s * k.astype(BF16).astype(F32)
         hi = w.astype(BF16)
         lo = (w - hi.astype(F32)).astype(BF16)
@@ -258,89 +265,89 @@
         m = s * k
         return t, sum(m[:, 128 * h:128 * (h + 1)] for h in range((c1 - c0) // 128))
 
-    acc[ORDER[0]], fold[...] = sums(lax.rem(y + ORDER[0], SIDE), 0, 3 * COLS)
+    acc[ORDER[0]], fold[...] = sums(lax.rem(own_v + ORDER[0], SIDE), 0, 3 * COLS)
     near(3)
 
     lane32 = lax.broadcasted_iota(I32, (SHARD, 128), 1)
     sub32 = lax.broadcasted_iota(I32, (SHARD, 128), 0)
 
     def spot(step):
-        return pl.ds(lax.rem(x + step, SIDE) * SHARD, SHARD)
-
-    def send_to(src, dst, sem, dx, dy, kind):
+        return pl.ds(lax.rem(own_u + step, SIDE) * SHARD, SHARD)
+
+    def send_to(src, dst, sem, du, dv, kind):
         pltpu.make_async_remote_copy(src_ref=src, dst_ref=dst, send_sem=sent.at[kind], recv_sem=sem,
-                                     device_id=peer(dx, dy), device_id_type=MESH).start()
+                                     device_id=peer(du, dv), device_id_type=MESH).start()
 
     i = 0
-    for dy in ORDER:
-        if dy == ORDER[0]:
-            t, m = sums(lax.rem(y + dy, SIDE), 3 * COLS, 4 * COLS)
-            t, m = t + acc[dy], m + fold[...]
+    for dv in ORDER:
+        if dv == ORDER[0]:
+            t, m = sums(lax.rem(own_v + dv, SIDE), 3 * COLS, 4 * COLS)
+            t, m = t + acc[dv], m + fold[...]
         else:
-            t, m = sums(lax.rem(y + dy, SIDE), 0, 4 * COLS)
-        acc[dy] = t
-        if dy:
-            send_y[dy - 1] = t[:, CUT:].astype(BF16)
-            send_to(send_y.at[dy - 1], recv_y.at[dy - 1], r_recv.at[4], 0, dy, 4)
-        for dx in HOPS:
-            send_x[dx - 1, dy] = acc[dy, spot(dx), :CUT].astype(BF16)
-            send_to(send_x.at[dx - 1, dy], recv_x.at[dx - 1, dy], r_recv.at[dy], dx, 0, 3)
+            t, m = sums(lax.rem(own_v + dv, SIDE), 0, 4 * COLS)
+        acc[dv] = t
+        if dv:
+            send_v[dv - 1] = t[:, CUT:].astype(BF16)
+            send_to(send_v.at[dv - 1], recv_v.at[dv - 1], r_recv.at[4], 0, dv, 4)
+        for du in HOPS:
+            send_u[du - 1, dv] = acc[dv, spot(du), :CUT].astype(BF16)
+            send_to(send_u.at[du - 1, dv], recv_u.at[du - 1, dv], r_recv.at[dv], du, 0, 3)
         m = jnp.sum(m, axis=1, keepdims=True)
-        mass[dy] = jnp.sum(jnp.where(sub128 == lane128, m, 0.0), axis=0, keepdims=True)
-        for dx in ORDER:
-            if (dx, dy) != (0, 0):
-                send_to(mass.at[dy], mass.at[SIDE + i], a_recv.at[0], dx, dy, 5)
+        mass[dv] = jnp.sum(jnp.where(sub128 == lane128, m, 0.0), axis=0, keepdims=True)
+        for du in ORDER:
+            if (du, dv) != (0, 0):
+                send_to(mass.at[dv], mass.at[SIDE + i], a_recv.at[0], du, dv, 5)
                 i += 1
 
     def come(ref, sem):
         pltpu.make_async_copy(ref, ref, sem).wait()
 
-    def first_x(dy):
-        come(recv_x.at[:, dy], r_recv.at[dy])
-        v = acc[dy, spot(0), :CUT]
+    def first_u(dv):
+        come(recv_u.at[:, dv], r_recv.at[dv])
+        r = acc[dv, spot(0), :CUT]
         for k in range(SIDE - 1):
-            v = v + recv_x[k, dy].astype(F32)
-        return v
-
-    def along_y(dy):
-        last_y[dy - 1] = first_x(dy)
-        send_to(last_y.at[dy - 1], last_y.at[SIDE - 2 + dy], r_recv.at[6], 0, dy, 7)
-
-    along_y(2)
-    along_y(1)
-    come(recv_y, r_recv.at[4])
-    v = acc[0, :, CUT:]
+            r = r + recv_u[k, dv].astype(F32)
+        return r
+
+    def along_v(dv):
+        last_v[dv - 1] = first_u(dv)
+        send_to(last_v.at[dv - 1], last_v.at[SIDE - 2 + dv], r_recv.at[6], 0, dv, 7)
+
+    along_v(2)
+    along_v(1)
+    come(recv_v, r_recv.at[4])
+    r = acc[0, :, CUT:]
     for k in range(SIDE - 1):
-        v = v + recv_y[k].astype(F32)
-    sum_y[...] = v
-    for dx in HOPS:
-        last_x[dx - 1] = sum_y[spot(dx)]
-        send_to(last_x.at[dx - 1], last_x.at[SIDE - 2 + dx], r_recv.at[5], dx, 0, 6)
-    along_y(3)
-    v = first_x(0)
+        r = r + recv_v[k].astype(F32)
+    sum_v[...] = r
+    for du in HOPS:
+        last_u[du - 1] = sum_v[spot(du)]
+        send_to(last_u.at[du - 1], last_u.at[SIDE - 2 + du], r_recv.at[5], du, 0, 6)
+    along_v(3)
+    r = first_u(0)
     a = mass[0]
     got = mass.at[pl.ds(SIDE, len(PEERS))]
     come(got, a_recv.at[0])
     for k in range(len(PEERS)):
         a = a + mass[SIDE + k]
-    m = jnp.sum(jnp.where(lane32 == x * SHARD + sub32, a, 0.0), axis=1, keepdims=True)
+    m = jnp.sum(jnp.where(lane32 == own_u * SHARD + sub32, a, 0.0), axis=1, keepdims=True)
     m = jnp.log(1.0 + m)
     log_ref[...] = jnp.sum(jnp.where(sub32 == lane32, m, 0.0), axis=0, keepdims=True)
-    w = sum_y[spot(0)]
-    there_x = last_x.at[pl.ds(SIDE - 1, SIDE - 1)]
-    there_y = last_y.at[pl.ds(SIDE - 1, SIDE - 1)]
-    come(there_x, r_recv.at[5])
+    w = sum_v[spot(0)]
+    there_u = last_u.at[pl.ds(SIDE - 1, SIDE - 1)]
+    there_v = last_v.at[pl.ds(SIDE - 1, SIDE - 1)]
+    come(there_u, r_recv.at[5])
     for k in range(SIDE - 1):
-        w = w + last_x[SIDE - 1 + k]
+        w = w + last_u[SIDE - 1 + k]
     out_ref[:, CUT:] = w
-    come(there_y, r_recv.at[6])
+    come(there_v, r_recv.at[6])
     for k in range(SIDE - 1):
-        v = v + last_y[SIDE - 1 + k]
-    out_ref[:, :CUT] = v
+        r = r + last_v[SIDE - 1 + k]
+    out_ref[:, :CUT] = r
     shards = cols.at[pl.ds(0, (OWNERS - 1) * SHARD)]
     counted = cm.at[pl.ds(0, OWNERS - 1)]
-    for what, sem in ((shards, sent.at[0]), (shards, sent.at[1]), (counted, sent.at[2]), (recv_x, sent.at[3]),
-                      (recv_y, sent.at[4]), (got, sent.at[5]), (there_x, sent.at[6]), (there_y, sent.at[7]),
+    for what, sem in ((shards, sent.at[0]), (shards, sent.at[1]), (counted, sent.at[2]), (recv_u, sent.at[3]),
+                      (recv_v, sent.at[4]), (got, sent.at[5]), (there_u, sent.at[6]), (there_v, sent.at[7]),
                       (mates, m_sem.at[0])):
         come(what, sem)
 
@@ -355,7 +362,6 @@
         block_sizes.reshape(1, 128),
         jnp.pad(fetch_blocks.reshape(1, OWNERS), room),
         jnp.pad(jnp.swapaxes(partners, 2, 3).reshape(4, OWNERS), room),
-        jnp.zeros((2, 128), I32),
     ]).astype(F32)
     out, logs = pl.pallas_call(
         kernel,

time: 47.6 us -> 47.1 us (0.989)
  no operation moved by 1% of the time
where the time goes in v4:
time: 47.1 us; the launch traced here: 47 us
  Pallas kernels  44.5 us (94%)
  local copies, waits for them, and re-layouts  1.15 us (2%)
  other arithmetic  0.71 us (2%)
  between operations  0.64 us (1%)
    pallas_call x1, Pallas kernels, body(): pl.pallas_call(kernel, out_shape=(jax.ShapeDtypeStruct((SHARD, WIDTH), F3...  44.5 us

profile of v4, /device:TPU:1, one launch (start us, length us, event | category | flops | bytes accessed | tf_op | source)
XLA Modules:
  0.0 47.0 jit_solution(767520298616027892)
XLA Ops:
  0.6 0.7 %fusion.ints = f32[6,128]{1,0:T(8,128)S(1)} fusion(s32[4,16]{1,0:T(4,128)} %bitcast.8, s32[1,16]{1,0:T(1,128)} %bitcast.9, s32[1,128]{1,0:T(1,128)} %bitcast.10), kind=kLoop, calls=%fused_computation.1 | loop fusion | flops 2304 | bytes 3904 | tf_op jit(solution)/shard_map/convert_element_type | solution.py:365
  1.3 44.5 %shard_map.59 = (f32[32,768]{1,0:T(8,128)S(1)}, f32[1,128]{1,0:T(1,128)S(1)}) custom-call(bf16[16,2,32,768]{3,2,1,0:T(8,128)(2,1)} %bitcast.11, f32[6,128]{1,0:T(8,128)S(1)} %fusion.ints), custom_call_target="tpu_custom_call" | custom-call | flops 2415919104 | bytes 4194304 | tf_op jit(solution)/shard_map/pallas_call | solution.py:366
  45.8 0.5 %slice_bitcast_fusion = f32[32]{0:T(128)} fusion(f32[1,128]{1,0:T(1,128)S(1)} %get-tuple-element.5), kind=kLoop, calls=%fused_computation.3 | loop fusion | bytes 256 | tf_op jit(solution)/shard_map/squeeze | solution.py:401
  46.4 0.6 %copy.7 = f32[32,768]{1,0:T(8,128)} copy(f32[32,768]{1,0:T(8,128)S(1)} %get-tuple-element.8) | data formatting | bytes 196608

commit v5 on v4

--- a/solution.py
+++ b/solution.py
@@ -19,7 +19,7 @@
 COLS = GROUP * PAIR
 FAR = 1e30
 
-KIDS = {0: (2, 1), 2: (5, 3), 5: (8, 7, 4, 6)}
+KIDS = {0: (2, 1), 2: (5, 3), 5: (7, 8, 6, 4)}
 SLOTS = (0, 2, -2, 1, -1, 5, -5, 3, -3, 8, 7, -7, 4, -4, 6, -6)
 SLOT = {d: s for s, d in enumerate(SLOTS)}
 SLOT[-8] = SLOT[8]

time: 47.1 us -> 47.1 us (level)
  no operation moved by 1% of the time
where the time goes in v5:
time: 47.1 us; the launch traced here: 46.9 us
  Pallas kernels  44.4 us (94%)
  local copies, waits for them, and re-layouts  1.15 us (2%)
  other arithmetic  0.71 us (2%)
  between operations  0.64 us (1%)
    pallas_call x1, Pallas kernels, body(): pl.pallas_call(kernel, out_shape=(jax.ShapeDtypeStruct((SHARD, WIDTH), F3...  44.4 us

profile of v5, /device:TPU:1, one launch (start us, length us, event | category | flops | bytes accessed | tf_op | source)
XLA Modules:
  0.0 46.9 jit_solution(14665643513775978250)
XLA Ops:
  0.6 0.7 %fusion.ints = f32[6,128]{1,0:T(8,128)S(1)} fusion(s32[4,16]{1,0:T(4,128)} %bitcast.8, s32[1,16]{1,0:T(1,128)} %bitcast.9, s32[1,128]{1,0:T(1,128)} %bitcast.10), kind=kLoop, calls=%fused_computation.1 | loop fusion | flops 2304 | bytes 3904 | tf_op jit(solution)/shard_map/convert_element_type | solution.py:365
  1.3 44.4 %shard_map.59 = (f32[32,768]{1,0:T(8,128)S(1)}, f32[1,128]{1,0:T(1,128)S(1)}) custom-call(bf16[16,2,32,768]{3,2,1,0:T(8,128)(2,1)} %bitcast.11, f32[6,128]{1,0:T(8,128)S(1)} %fusion.ints), custom_call_target="tpu_custom_call" | custom-call | flops 2415919104 | bytes 4194304 | tf_op jit(solution)/shard_map/pallas_call | solution.py:366
  45.8 0.5 %slice_bitcast_fusion = f32[32]{0:T(128)} fusion(f32[1,128]{1,0:T(1,128)S(1)} %get-tuple-element.5), kind=kLoop, calls=%fused_computation.3 | loop fusion | bytes 256 | tf_op jit(solution)/shard_map/squeeze | solution.py:401
  46.3 0.6 %copy.7 = f32[32,768]{1,0:T(8,128)} copy(f32[32,768]{1,0:T(8,128)S(1)} %get-tuple-element.8) | data formatting | bytes 196608
